TPU v7x, 32 devices: a whole 2x2x4 slice. The times are simulated.
32 devices in a mesh: pair: 8 (over z, x), virt: 4 (over y, core).
Axes of the slice: x: 2, y: 2, z: 4, core: 2. Of those that a mesh axis runs over, the one named last changes fastest.
Arguments:
- amps: bfloat16 [1792, 480, 480], P('pair', 'virt'), may hold values from -6 to 6
- integrals: bfloat16 [2304, 230400], P(None, ('virt', 'pair')), may hold values from -0.01171875 to 0.01171875
- slot_pair: int32 [1792], P('pair'), may hold values from -1 to 1175, as said below
- occ_energy: float32 [48], replicated, may hold values from -1.2 to -0.4
- virt_energy: float32 [48], replicated, may hold values from 0.3 to 1.5
Outputs:
- update: float32 [1792, 48, 48], P('pair', 'virt')
Inputs may be any that keep to these rules, and one draw needn't show every extreme that they name: `slot_pair`: each of the 1176 pairs i <= j stands in exactly one slot, -1 marks an empty slot; the 224 slots of one index of pair hold uneven numbers of pairs, and some index has all 224 filled.
All inputs are finite; a program needn't handle non-finite values.
Results may differ from a plain program's by a relative error of at most 0.0003.
Values may be sent and summed in bfloat16 or wider, within the bound.
A program may use at most 192 MiB of HBM per device.

v0:
```python
import jax
import jax.numpy as jnp
from jax import lax
from jax.sharding import PartitionSpec as P


def pair_energy(slot_pair, occ_energy):
    nocc_count = occ_energy.shape[0]
    orbital = jnp.arange(nocc_count, dtype=jnp.int32)
    starts_row = orbital * nocc_count - orbital * (orbital - 1) // 2
    row_index = jnp.sum((starts_row[None, 1:] <= slot_pair[:, None]).astype(jnp.int32), axis=1)
    same_row = orbital[None, :] == row_index[:, None]
    row_start = jnp.sum(jnp.where(same_row, starts_row[None, :], 0), axis=1)
    column_index = slot_pair - row_start + row_index
    first_energy = jnp.sum(
        jnp.where(same_row, occ_energy[None, :], jnp.zeros_like(occ_energy)[None, :]), axis=1
    )
    same_column = orbital[None, :] == column_index[:, None]
    second_energy = jnp.sum(
        jnp.where(same_column, occ_energy[None, :], jnp.zeros_like(occ_energy)[None, :]), axis=1
    )
    return (first_energy + second_energy, slot_pair >= 0)


def ladder_term(row_block, columns):
    partial_value = lax.dot_general(
        row_block, columns, (((1,), (1,)), ((), ())), preferred_element_type=jnp.float32
    )
    return partial_value


def body(amps, integrals, slot_pair, occ_energy, virt_energy):
    slot_count = amps.shape[0]
    local_width = amps.shape[1] * amps.shape[2]
    flattened = amps.reshape(slot_count, local_width)
    window = virt_energy.shape[0]
    virt_count = lax.axis_size("virt")
    local_rows = window // virt_count
    panels = lax.all_to_all(flattened, "pair", split_axis=1, concat_axis=0, tiled=True)
    owned = lax.psum_scatter(
        ladder_term(panels, integrals), "pair", scatter_dimension=0, tiled=True
    )
    owned = lax.psum_scatter(
        owned.reshape(slot_count, window, window), "virt", scatter_dimension=1, tiled=True
    )
    flipped = lax.all_to_all(owned, "virt", split_axis=2, concat_axis=1, tiled=True)
    residual = owned + jnp.transpose(flipped, (0, 2, 1))
    pair_sum, filled = pair_energy(slot_pair, occ_energy)
    local_energy = lax.dynamic_slice_in_dim(
        virt_energy, lax.axis_index("virt") * local_rows, local_rows
    )
    denominator = pair_sum[:, None, None] - local_energy[None, :, None] - virt_energy[None, None, :]
    return jnp.where(filled[:, None, None], residual / denominator, jnp.zeros_like(residual))


def solution(mesh):
    placed = (P("pair", "virt", None), P(None, ("virt", "pair")), P("pair"), P(), P())
    return jax.shard_map(
        body, mesh=mesh, in_specs=placed, out_specs=P("pair", "virt", None), check_vma=False
    )
```

profile of v0, /device:TPU:0, one launch (start us, length us, event | category | flops | bytes accessed | tf_op | source)
XLA Modules:
  0.0 1047.2 jit_solution(129993925691351900)
XLA Ops:
  6.5 0.0 reduce-scatter.3.cloned.1.call-start
  6.5 43.7 %all_to_all.27 = bf16[224,8,7200]{2,1,0:T(8,128)(2,1)} reshape(bf16[224,120,480]{2,1,0:T(8,128)(2,1)} %param.5) | data formatting | bytes 51609600 | tf_op jit(solution)/shard_map/all_to_all | solution.py:39
  50.2 15.1 %copy.16 = bf16[224,8,7200]{2,0,1:T(8,128)(2,1)S(1)} copy(bf16[224,8,7200]{2,1,0:T(8,128)(2,1)} %all_to_all.27) | data formatting | bytes 51609600 | tf_op jit(solution)/shard_map/all_to_all | solution.py:39
  65.4 570.9 %all_to_all.37 = bf16[224,8,7200]{2,0,1:T(8,128)(2,1)} all-to-all(bf16[224,8,7200]{2,0,1:T(8,128)(2,1)S(1)} %copy.16), channel_id=1, replica_groups=mesh['pair'=8,'virt'=4] {'pair'}, dimensions={1} | all-to-all | bytes 51609600 | tf_op jit(solution)/shard_map/all_to_all | solution.py:39
  636.3 0.0 copy-start.1
  636.3 0.0 copy-start
  636.3 0.0 copy-start.2
  636.3 72.4 %fusion.3 = f32[1792,2304]{1,0:T(8,128)} fusion(bf16[1792,7200]{1,0:T(8,128)(2,1)} %bitcast.18, bf16[2304,7200]{0,1:T(8,128)(2,1)} %param.6), kind=kOutput, calls=%fused_computation.20 | convolution fusion | flops 59454259200 | bytes 75497472 | tf_op jit(solution)/shard_map/dot_general | solution.py:26
  708.7 0.0 reduce-scatter.3.cloned.1.call-update
  708.8 0.0 reduce-scatter.5.cloned.1.call-start
  708.8 276.7 %reduce-scatter.3.cloned.1.call-done = f32[224,2304]{1,0:T(8,128)} async-done(((f32[1792,2304]{1,0:T(8,128)}), f32[224,2304]{1,0:T(8,128)}) %reduce-scatter.3.cloned.1.call-update) | async-done | bytes 2064400 | tf_op jit(solution)/shard_map/reduce_scatter | solution.py:40
  985.5 3.0 copy.17
  988.5 0.0 reduce-scatter.5.cloned.1.call-update
  988.6 0.1 slice.3
  988.6 0.0 copy-done.1
  988.6 0.1 dynamic_slice.3
  988.7 0.0 copy-done
  988.7 0.1 convert_reduce_fusion
  988.8 0.1 select_reduce_fusion.1
  988.9 0.0 copy-done.2
  988.9 0.1 select_reduce_fusion
  989.0 31.7 %reduce-scatter.5.cloned.1.call-done = f32[224,12,48]{0,2,1:T(8,128)} async-done(((f32[224,48,48]{0,2,1:T(8,128)}), f32[224,12,48]{0,2,1:T(8,128)}) %reduce-scatter.5.cloned.1.call-update) | async-done | bytes 516112 | tf_op jit(solution)/shard_map/reduce_scatter | solution.py:43
  1020.8 2.3 copy.18
  1023.1 3.5 all-to-all-start.1
  1026.6 0.1 broadcast_subtract_fusion
  1026.6 11.5 %all-to-all-done.1 = f32[224,12,48]{0,1,2:T(8,128)S(1)} async-done(((f32[224,12,48]{0,1,2:T(8,128)}), f32[224,12,48]{0,1,2:T(8,128)S(1)}, u32[]{:S(2)}, u32[]{:S(2)}) %all-to-all-start.1) | async-done | bytes 516128 | tf_op jit(solution)/shard_map/all_to_all | solution.py:46
  1038.2 0.1 copy.20
  1038.3 0.1 all_to_all.34
  1038.3 2.0 fusion.1
  (4 shorter events, 0.0 us)
Async XLA Ops:
  6.5 979.0 %reduce-scatter.3.cloned.1.call-start = ((), (), s32[]{:S(2)}) async-start(), calls=%async_computation.4 | async-start | bytes 18579456 | tf_op jit(solution)/shard_map/reduce_scatter | solution.py:40
  636.3 352.3 %copy-start.1 = (f32[48]{0:T(128)S(1)}, f32[48]{0:T(128)}, u32[]{:S(2)}) copy-start(f32[48]{0:T(128)} %param.9) | copy-start | bytes 580
  636.3 352.4 %copy-start = (s32[224]{0:T(256)S(1)}, s32[224]{0:T(256)}, u32[]{:S(2)}) copy-start(s32[224]{0:T(256)} %param.7) | copy-start | bytes 2692
  636.3 352.6 %copy-start.2 = (f32[48]{0:T(128)S(1)}, f32[48]{0:T(128)}, u32[]{:S(2)}) copy-start(f32[48]{0:T(128)} %param.8) | copy-start | bytes 580
  708.8 312.0 %reduce-scatter.5.cloned.1.call-start = ((), (), s32[]{:S(2)}) async-start(), calls=%async_computation.5 | async-start | bytes 2949120 | tf_op jit(solution)/shard_map/reduce_scatter | solution.py:43
  1023.1 15.1 %all-to-all-start.1 = ((f32[224,12,48]{0,1,2:T(8,128)}), f32[224,12,48]{0,1,2:T(8,128)S(1)}, u32[]{:S(2)}, u32[]{:S(2)}) async-start(f32[224,12,48]{0,1,2:T(8,128)} %copy.18), calls=%async_computation.3 | async-start | bytes 1572864 | tf_op jit(solution)/shard_map/all_to_all | solution.py:46
Sparse Core Ops, SparseCore 0:
  708.9 276.5 reduce-scatter.2
  988.7 32.0 reduce-scatter.4
where the time goes:
time: 1050 us
  blocking collectives  571 us (54%)
  waiting for transfers between devices  320 us (30%)
  matrix products  72.4 us (7%)
  local copies, waits for them, and re-layouts  64.4 us (6%)
  between operations  13.5 us (1%)
    all_to_all x1, blocking collectives, body(): lax.all_to_all(flattened, 'pair', split_axis=1, concat_axis=0, tiled=True)  571 us
    reduce_scatter x1, waiting for transfers between devices, body(): lax.psum_scatter(ladder_term(panels, integrals), 'pair', scatter_dimensio...  277 us
    dot_general x1, matrix products, ladder_term(): lax.dot_general(row_block, columns, (((1,), (1,)), ((), ())), preferred_e...  72.4 us
    all_to_all x2, local copies, waits for them, and re-layouts, body(): lax.all_to_all(flattened, 'pair', split_axis=1, concat_axis=0, tiled=True)  58.8 us
    reduce_scatter x1, waiting for transfers between devices, body(): lax.psum_scatter(owned.reshape(slot_count, window, window), 'virt', scatt...  31.7 us
  transfers between devices with their start and end apart: 3, of which 3 were waited for; matrix products, arithmetic and copies ran while one was open for 0% of the time, Pallas kernels for 0%

commit v1 on v0

--- a/solution.py
+++ b/solution.py
@@ -1,6 +1,10 @@
+import functools
+
 import jax
 import jax.numpy as jnp
 from jax import lax
+from jax.experimental import pallas as pl
+from jax.experimental.pallas import tpu as pltpu
 from jax.sharding import PartitionSpec as P
 
 
@@ -53,8 +57,252 @@
     return jnp.where(filled[:, None, None], residual / denominator, jnp.zeros_like(residual))
 
 
+ROWS = 32
+TILE = 256
+LANES = 128
+
+
+def exchange_kernel(count, fold, window, send, integrals, update, landed, crossed, weights, panel,
+                    stage, folded, arrived, total, turned, returned, send_sem, recv_sem, load_sem,
+                    panel_sem, cross_send, cross_recv, arrived_sem, back_send, back_recv):
+    me = lax.axis_index("pair")
+    chunks = send.shape[0]
+    halves = stage.shape[0]
+    column = lax.axis_index("virt")
+    local = window // fold
+    barrier = pltpu.get_barrier_semaphore()
+    for step in range(1, count):
+        pl.semaphore_signal(
+            barrier, inc=1, device_id={"pair": lax.rem(me + step, count)},
+            device_id_type=pl.DeviceIdType.MESH,
+        )
+    for step in range(1, fold):
+        pl.semaphore_signal(
+            barrier, inc=1, device_id={"virt": lax.rem(column + step, fold)},
+            device_id_type=pl.DeviceIdType.MESH,
+        )
+    pl.semaphore_wait(barrier, count + fold - 2)
+
+    def remote(index, step):
+        target = lax.rem(me + step, count)
+        return pltpu.make_async_remote_copy(
+            src_ref=send.at[index, target],
+            dst_ref=landed.at[index, pl.ds(pl.multiple_of(me * ROWS, ROWS), ROWS)],
+            send_sem=send_sem.at[index, step - 1],
+            recv_sem=recv_sem.at[index, step - 1],
+            device_id={"pair": target},
+            device_id_type=pl.DeviceIdType.MESH,
+        )
+
+    def start(index):
+        for step in range(1, count):
+            remote(index, step).start()
+
+    def landing(index, step):
+        origin = lax.rem(me + count - step, count)
+        return pltpu.make_async_remote_copy(
+            src_ref=send.at[index, origin],
+            dst_ref=landed.at[index, pl.ds(pl.multiple_of(origin * ROWS, ROWS), ROWS)],
+            send_sem=send_sem.at[index, step - 1],
+            recv_sem=recv_sem.at[index, step - 1],
+            device_id={"pair": origin},
+            device_id_type=pl.DeviceIdType.MESH,
+        )
+
+    def across(index, step):
+        target = lax.rem(column + step, fold)
+        return pltpu.make_async_remote_copy(
+            src_ref=folded.at[pl.ds(target * local, local)],
+            dst_ref=crossed.at[index, step - 1],
+            send_sem=cross_send.at[index, step - 1],
+            recv_sem=cross_recv.at[index, step - 1],
+            device_id={"virt": target},
+            device_id_type=pl.DeviceIdType.MESH,
+        )
+
+    def back(index, step):
+        target = lax.rem(me + step, count)
+        return pltpu.make_async_remote_copy(
+            src_ref=turned.at[pl.ds(pl.multiple_of(target * ROWS, ROWS), ROWS)],
+            dst_ref=returned.at[step, pl.ds(pl.multiple_of(index * ROWS, ROWS), ROWS)],
+            send_sem=back_send.at[index, step - 1],
+            recv_sem=back_recv.at[index, step - 1],
+            device_id={"pair": target},
+            device_id_type=pl.DeviceIdType.MESH,
+        )
+
+    total[...] = jnp.zeros_like(total)
+    start(0)
+    if chunks > 1:
+        start(1)
+    load = pltpu.make_async_copy(integrals, weights, load_sem)
+    load.start()
+    load.wait()
+
+    def one(index, carry):
+        for step in range(1, count):
+            landing(index, step).wait_recv()
+
+        @pl.when(index + 2 < chunks)
+        def _():
+            start(index + 2)
+
+        for step in range(count):
+            origin = lax.rem(me + count - step, count)
+            place = pl.ds(pl.multiple_of(origin * ROWS, ROWS), ROWS)
+            source = send.at[index, origin] if step == 0 else landed.at[index, place]
+            pltpu.make_async_copy(source, panel.at[place], panel_sem.at[step]).start()
+        for step in range(count):
+            origin = lax.rem(me + count - step, count)
+            place = pl.ds(pl.multiple_of(origin * ROWS, ROWS), ROWS)
+            source = send.at[index, origin] if step == 0 else landed.at[index, place]
+            pltpu.make_async_copy(source, panel.at[place], panel_sem.at[step]).wait()
+
+        def columns(tile, inner):
+            place = pl.ds(pl.multiple_of(tile * TILE, TILE), TILE)
+            term = jnp.dot(panel[...], weights[:, place], preferred_element_type=jnp.float32)
+            for half in range(halves):
+                stage[half, place, :] = term[half * LANES:(half + 1) * LANES].T
+            return inner
+
+        lax.fori_loop(0, stage.shape[1] // TILE, columns, 0)
+        for row in range(window):
+            for half in range(halves):
+                folded[row, :, half * LANES:(half + 1) * LANES] = (
+                    stage[half, row * window:(row + 1) * window, :]
+                    + stage[half, pl.ds(row, window, stride=window), :]
+                )
+        for step in range(1, fold):
+            across(index, step).start()
+        for step in range(1, fold):
+            across(index, step).wait_recv()
+        for step in range(1, fold):
+            pltpu.make_async_copy(
+                crossed.at[index, step - 1], arrived.at[step - 1], arrived_sem.at[step - 1]
+            ).start()
+        for step in range(1, fold):
+            pltpu.make_async_copy(
+                crossed.at[index, step - 1], arrived.at[step - 1], arrived_sem.at[step - 1]
+            ).wait()
+        for row in range(local):
+            value = folded[column * local + row]
+            for step in range(1, fold):
+                value = value + arrived[step - 1, row]
+            total[row * window:(row + 1) * window, :] = value
+
+        @pl.when(index > 0)
+        def _():
+            for step in range(1, count):
+                back(index - 1, step).wait_send()
+
+        for part in range(turned.shape[1] // LANES):
+            turned[:, part * LANES:(part + 1) * LANES] = total[part * LANES:(part + 1) * LANES, :].T
+        for step in range(1, count):
+            back(index, step).start()
+        mine = pl.ds(pl.multiple_of(me * ROWS, ROWS), ROWS)
+        returned[0, pl.ds(pl.multiple_of(index * ROWS, ROWS), ROWS), :] = turned[mine, :]
+        for step in range(1, fold):
+            across(index, step).wait_send()
+        for step in range(1, count):
+            remote(index, step).wait_send()
+        return carry
+
+    lax.fori_loop(0, chunks, one, 0)
+    for step in range(1, count):
+        back(chunks - 1, step).wait_send()
+
+    def gather(index, carry):
+        for step in range(1, count):
+            back(index, step).wait_recv()
+        place = pl.ds(pl.multiple_of(index * ROWS, ROWS), ROWS)
+        value = returned[0, place, :]
+        for step in range(1, count):
+            value = value + returned[step, place, :]
+        update[place, :] = value
+        return carry
+
+    lax.fori_loop(0, chunks, gather, 0)
+
+
+def exchanged_ladder(send, weights, window):
+    chunks, count, rows, width = send.shape
+    lanes = count * rows
+    fold = lax.axis_size("virt")
+    local = window // fold
+    padded = -(-local * window // LANES) * LANES
+    call = pl.pallas_call(
+        functools.partial(exchange_kernel, count, fold, window),
+        out_shape=(
+            jax.ShapeDtypeStruct((chunks * rows, padded), jnp.float32),
+            jax.ShapeDtypeStruct((chunks, lanes, width), send.dtype),
+            jax.ShapeDtypeStruct((chunks, fold - 1, local, window, lanes), jnp.float32),
+        ),
+        in_specs=[pl.BlockSpec(memory_space=pl.ANY)] * 2,
+        out_specs=(pl.BlockSpec(memory_space=pltpu.VMEM),) + (pl.BlockSpec(memory_space=pl.ANY),) * 2,
+        scratch_shapes=[
+            pltpu.VMEM(weights.shape, weights.dtype),
+            pltpu.VMEM((lanes, width), send.dtype),
+            pltpu.VMEM((lanes // LANES, window * window, LANES), jnp.float32),
+            pltpu.VMEM((window, window, lanes), jnp.float32),
+            pltpu.VMEM((fold - 1, local, window, lanes), jnp.float32),
+            pltpu.VMEM((padded, lanes), jnp.float32),
+            pltpu.VMEM((lanes, padded), jnp.float32),
+            pltpu.VMEM((count, chunks * rows, padded), jnp.float32),
+            pltpu.SemaphoreType.DMA((chunks, count - 1)),
+            pltpu.SemaphoreType.DMA((chunks, count - 1)),
+            pltpu.SemaphoreType.DMA(()),
+            pltpu.SemaphoreType.DMA((count,)),
+            pltpu.SemaphoreType.DMA((chunks, fold - 1)),
+            pltpu.SemaphoreType.DMA((chunks, fold - 1)),
+            pltpu.SemaphoreType.DMA((fold - 1,)),
+            pltpu.SemaphoreType.DMA((chunks, count - 1)),
+            pltpu.SemaphoreType.DMA((chunks, count - 1)),
+        ],
+        compiler_params=pltpu.CompilerParams(
+            collective_id=1, has_side_effects=True, vmem_limit_bytes=58 * 2**20
+        ),
+        cost_estimate=pl.CostEstimate(
+            flops=2 * chunks * lanes * width * window * window,
+            bytes_accessed=2 * (weights.size + 3 * send.size), transcendentals=0,
+        ),
+    )
+    return call(send, weights)[0][:, :local * window]
+
+
+def overlapped_body(amps, integrals, slot_pair, occ_energy, virt_energy):
+    slot_count = amps.shape[0]
+    window = virt_energy.shape[0]
+    pair_count = lax.axis_size("pair")
+    virt_count = lax.axis_size("virt")
+    local_rows = window // virt_count
+    width = amps.shape[1] * amps.shape[2] // pair_count
+    groups = slot_count // ROWS
+    send = amps.reshape(groups, ROWS, pair_count, width).transpose(0, 2, 1, 3)
+    weights = integrals.T
+    residual = exchanged_ladder(send, weights, window)
+    residual = residual.reshape(slot_count, local_rows, window).transpose(1, 2, 0)
+    pair_sum, filled = pair_energy(slot_pair, occ_energy)
+    local_energy = lax.dynamic_slice_in_dim(
+        virt_energy, lax.axis_index("virt") * local_rows, local_rows
+    )
+    denominator = pair_sum[None, None, :] - local_energy[:, None, None] - virt_energy[None, :, None]
+    update = jnp.where(filled[None, None, :], residual / denominator, jnp.zeros_like(residual))
+    return jnp.transpose(update, (2, 0, 1))
+
+
+def chosen_body(amps, *rest):
+    slot_count = amps.shape[0]
+    window = rest[-1].shape[0]
+    lanes = lax.axis_size("pair") * ROWS
+    fits = (
+        slot_count % ROWS == 0 and slot_count // ROWS > 1 and lanes == 2 * LANES
+        and window * window % TILE == 0
+    )
+    return (overlapped_body if fits else body)(amps, *rest)
+
+
 def solution(mesh):
     placed = (P("pair", "virt", None), P(None, ("virt", "pair")), P("pair"), P(), P())
     return jax.shard_map(
-        body, mesh=mesh, in_specs=placed, out_specs=P("pair", "virt", None), check_vma=False
-    )
+        chosen_body, mesh=mesh, in_specs=placed, out_specs=P("pair", "virt", None), check_vma=False
+    )

time: 1050 us -> 781 us (0.74)
  Pallas kernels: 0 us -> 699 us
  blocking collectives: 571 us -> 0 us
  waiting for transfers between devices: 320 us -> 0 us
  matrix products: 72.4 us -> 0 us
  between operations: 13.5 us -> 0.05 us
    pallas_call x0 -> x1, Pallas kernels: none -> 699 us  [exchanged_ladder(): return call(send, weights)[0][:, :local * window]]
    all_to_all x1 -> x0, blocking collectives: 571 us -> none  [body(): lax.all_to_all(flattened, 'pair', split_axis=1, concat_axis=0, tiled=True)]
    reduce_scatter x2 -> x0, waiting for transfers between devices: 308 us -> none  [the longest x1 277 us: body(): lax.psum_scatter(ladder_term(panels, integrals), 'pair', scatter_dimensio...]
    dot_general x1 -> x0, matrix products: 72.4 us -> none  [ladder_term(): lax.dot_general(row_block, columns, (((1,), (1,)), ((), ())), preferred_e...]
    reshape x0 -> x2, local copies, waits for them, and re-layouts: none -> 67.4 us  [overlapped_body(): send = amps.reshape(groups, ROWS, pair_count, width).transpose(0, 2, 1, 3)]
    all_to_all x4 -> x0, local copies, waits for them, and re-layouts: 59 us -> none  [the longest x2 58.8 us: body(): lax.all_to_all(flattened, 'pair', split_axis=1, concat_axis=0, tiled=True)]
    all_to_all x1 -> x0, waiting for transfers between devices: 11.5 us -> none  [body(): lax.all_to_all(owned, 'virt', split_axis=2, concat_axis=1, tiled=True)]
  transfers between devices with their start and end apart: 3 -> 0, of which waited for: 3 -> 0; matrix products, arithmetic and copies ran while one was open for 0% -> 0% of each run, Pallas kernels for 0% -> 0%
where the time goes in v1:
time: 781 us; the launch traced here: 769 us
  Pallas kernels  699 us (90%)
  local copies, waits for them, and re-layouts  68.8 us (9%)
    pallas_call x1, Pallas kernels, exchanged_ladder(): return call(send, weights)[0][:, :local * window]  699 us
    reshape x2, local copies, waits for them, and re-layouts, overlapped_body(): send = amps.reshape(groups, ROWS, pair_count, width).transpose(0, 2, 1, 3)  67.4 us

profile of v1, /device:TPU:0, one launch (start us, length us, event | category | flops | bytes accessed | tf_op | source)
XLA Modules:
  0.0 769.3 jit_solution(6346246627997401203)
XLA Ops:
  0.0 43.6 %reshape.71 = bf16[7,32,8,7200]{3,2,1,0:T(8,128)(2,1)} reshape(bf16[224,120,480]{2,1,0:T(8,128)(2,1)} %param.5) | data formatting | bytes 51609600 | tf_op jit(solution)/shard_map/reshape | solution.py:280
  43.6 23.7 %copy.12 = bf16[7,32,8,7200]{3,1,2,0:T(8,128)(2,1)} copy(bf16[7,32,8,7200]{3,2,1,0:T(8,128)(2,1)} %reshape.71) | data formatting | bytes 51609600 | tf_op jit(solution)/shard_map/reshape | solution.py:280
  67.4 0.0 copy-start.1
  67.4 0.0 copy-start
  67.4 0.0 copy-start.2
  67.4 699.1 %shard_map.55 = (f32[224,640]{1,0:T(8,128)}, bf16[7,256,7200]{2,1,0:T(8,128)(2,1)}, f32[7,3,12,48,256]{4,3,2,1,0:T(8,128)}) custom-call(bf16[7,8,32,7200]{3,2,1,0:T(8,128)(2,1)} %bitcast.6, bf16[7200,2304]{1,0:T(8,128)(2,1)} %bitcast.9), custom_call_target="tpu_custom_call" | custom-call | flops 59454259200 | bytes 110592000 | tf_op jit(solution)/shard_map/pallas_call | solution.py:269
  766.4 1.3 copy.10
  767.7 0.0 copy-done.1
  767.7 0.1 dynamic_slice.3
  767.8 0.1 slice.7
  767.9 0.0 copy-done
  767.9 0.1 convert_reduce_fusion
  768.0 0.1 select_reduce_fusion.1
  768.1 0.0 copy-done.2
  768.1 0.1 select_reduce_fusion
  768.2 0.1 broadcast_subtract_fusion
  768.3 1.0 divide_select_fusion
  (4 shorter events, 0.0 us)
Async XLA Ops:
  67.4 700.4 %copy-start.1 = (f32[48]{0:T(128)S(1)}, f32[48]{0:T(128)}, u32[]{:S(2)}) copy-start(f32[48]{0:T(128)} %param.9) | copy-start | bytes 580
  67.4 700.5 %copy-start = (s32[224]{0:T(256)S(1)}, s32[224]{0:T(256)}, u32[]{:S(2)}) copy-start(s32[224]{0:T(256)} %param.7) | copy-start | bytes 2692
  67.4 700.7 %copy-start.2 = (f32[48]{0:T(128)S(1)}, f32[48]{0:T(128)}, u32[]{:S(2)}) copy-start(f32[48]{0:T(128)} %param.8) | copy-start | bytes 580
